TPU v7x, 256 devices: a whole 4x4x8 slice. The times are simulated.
256 devices in a mesh: dir: 64 (over x, z, core), box: 4 (over y).
Axes of the slice: x: 4, y: 4, z: 8, core: 2. Of those that a mesh axis runs over, the one named last changes fastest.
Arguments:
- wedge_local: bfloat16 [4096, 64, 256], P('box', 'dir'), may hold values from -6 to 6
- wedge_ops: bfloat16 [16384, 512], P(('dir', 'box')), may hold values from -0.046875 to 0.046875
- octant_angle: float32 [8, 64, 128], replicated, may hold values from -3.140625 to 3.140625
- child_box: int32 [49152], P(('box', 'dir')), may hold values from -1 to 32767, as said below
Outputs:
- child_local: bfloat16 [49152, 512], P(('box', 'dir'))
Inputs may be any that keep to these rules, and one draw needn't show every extreme that they name: `child_box`: taking the slots in blocks of 192 (block j = b * 64 + d for box range b), block j holds consecutive Morton child indices from its first slot on and -1 after them; the blocks of box range b together hold every child of parents b * 16 * 64 to (b + 1) * 16 * 64 - 1 once, in order, and the children of block j have parents within 4 boxes of parents (b * 64 + d) * 16 to (b * 64 + d + 1) * 16 - 1. Every draw fills some block completely.
All inputs are finite; a program needn't handle non-finite values.
Results may differ from a plain program's by a relative error of at most 0.0049.
Values may be sent and summed in bfloat16 or wider, within the bound.
A program may use at most 128 MiB of HBM per device.

v0:
```python
import jax
import jax.numpy as jnp
from jax import lax
from jax.sharding import PartitionSpec as P


def with_halo(array, sides, width):
    for axis, dim in sides:
        peers, length = (lax.axis_size(axis), array.shape[dim])
        up = [(i, (i + 1) % peers) for i in range(peers - 1)]
        down = [(j, i) for i, j in up]
        last = lax.slice_in_dim(array, length - width, length, axis=dim)
        initial = lax.slice_in_dim(array, 0, width, axis=dim)
        before = lax.ppermute(last, axis, up)
        after = lax.ppermute(initial, axis, down)
        array = jnp.concatenate([before, array, after], axis=dim)
    return array


def rotate(values, angles):
    halves = values.shape[-1] // 2
    real_part = values[..., :halves]
    imag_part = values[..., halves:]
    cosine = jnp.cos(angles)
    sine_vals = jnp.sin(angles)
    return jnp.concatenate(
        [real_part * cosine - imag_part * sine_vals, real_part * sine_vals + imag_part * cosine],
        axis=-1,
    )


def on_device(wedge_local, wedge_ops, octant_angle, child_box):
    dir_count = lax.axis_size("dir")
    dir_index = lax.axis_index("dir")
    box_index = lax.axis_index("box")
    quarter = wedge_local.shape[0]
    par_dev = quarter // dir_count
    margin = par_dev // 4
    wedges = octant_angle.shape[1]
    width = wedge_local.shape[2]
    first_parent = box_index * quarter + dir_index * par_dev - margin
    occupied = child_box >= 0
    target = jnp.where(occupied, child_box, 0)
    grouped = lax.all_to_all(wedge_local, "dir", split_axis=0, concat_axis=1, tiled=True)
    widened = with_halo(grouped, (("dir", 0),), margin)
    local_parent = jnp.clip(target // 8 - first_parent, 0, widened.shape[0] - 1)
    picked = widened[local_parent]
    octant = target % 8
    selector = (octant[:, None] == jnp.arange(8, dtype=jnp.int32)[None, :]).astype(jnp.float32)
    angle_table = octant_angle.reshape(8, -1)
    slot_angle = jnp.dot(selector, angle_table, precision=lax.Precision.HIGHEST).reshape(
        -1, wedges, width // 2
    )
    shifted = rotate(picked.astype(jnp.float32), slot_angle).astype(jnp.bfloat16)
    operand = shifted.reshape(picked.shape[0], -1)
    result = jnp.dot(
        operand,
        lax.all_gather(wedge_ops, ("dir", "box"), axis=0, tiled=True),
        preferred_element_type=jnp.float32,
    )
    return jnp.where(occupied[:, None], result, 0.0).astype(jnp.bfloat16)


def solution(mesh):
    placed = (P("box", "dir", None), P(("dir", "box"), None), P(), P(("box", "dir")))
    return jax.shard_map(
        on_device, mesh=mesh, in_specs=placed, out_specs=P(("box", "dir"), None), check_vma=False
    )
```

profile of v0, /device:TPU:1, one launch (start us, length us, event | category | flops | bytes accessed | tf_op | source)
XLA Modules:
  0.0 158.7 jit_solution(9470784577099611418)
XLA Ops:
  6.5 0.0 all-gather.2.cloned.1.call-start
  6.5 0.7 all-gather.2.cloned.1.call-update
  7.3 0.5 broadcast.51
  7.8 2.1 %reduce = bf16[1024,256]{1,0:T(8,128)(2,1)S(1)} reduce(bf16[1024,1,256]{2,0,1:T(8,128)(2,1)} %param.4, bf16[]{:T(256)} %broadcast.51), dimensions={1}, to_apply=%copy.10.reduce_sub_computation | reduce | bytes 1048578 | tf_op args[0]
  9.8 0.9 reshape.23
  10.8 13.0 %all-to-all-start = ((bf16[64,2,2048]{2,1,0:T(2,128)(2,1)}), bf16[64,2,2048]{2,1,0:T(2,128)(2,1)S(1)}, u32[]{:S(2)}, u32[]{:S(2)}) async-start(bf16[64,2,2048]{2,1,0:T(2,128)(2,1)} %reshape.23), calls=%async_computation | async-start | bytes 1048576 | tf_op jit(solution)/shard_map/all_to_all | solution.py:44
  23.8 0.7 compare_select_fusion
  24.5 0.0 copy-start
  24.5 29.7 %fusion.6 = (f32[192,64,128]{2,0,1:T(8,128)}, f32[192,64,128]{2,0,1:T(8,128)}) fusion(f32[1,8,64,128]{3,2,1,0:T(8,128)} %bitcast.44, s32[192]{0:T(256)S(1)} %get-tuple-element.14), kind=kOutput, calls=%fused_computation.29 | convolution fusion | flops 150996480 | bytes 12845824 | tf_op jit(solution)/shard_map/dot_general | solution.py:51
  54.2 0.0 all-to-all-done
  54.2 0.5 reshape.24
  54.8 0.1 copy.14
  54.8 0.2 copy.27
  55.0 3.5 %collective-permute-start = (bf16[4,64,256]{2,1,0:T(8,128)(2,1)S(1)}, bf16[4,64,256]{2,1,0:T(8,128)(2,1)S(1)}, u32[]{:S(2)}, u32[]{:S(2)}) collective-permute-start(bf16[4,64,256]{2,1,0:T(8,128)(2,1)S(1)} %get-tuple-element.9), channel_id=1, source_target_pairs={{0,4},{4,8},{8,12},{12,16},{16,20},{20,24},{24,28},{28,32},{32,36}... | collective-permute-start | bytes 393224 | tf_op jit(solution)/shard_map/ppermute | solution.py:14
  58.6 2.1 %collective-permute-start.1 = (bf16[4,64,256]{2,1,0:T(8,128)(2,1)S(1)}, bf16[4,64,256]{2,1,0:T(8,128)(2,1)S(1)}, u32[]{:S(2)}, u32[]{:S(2)}) collective-permute-start(bf16[4,64,256]{2,1,0:T(8,128)(2,1)S(1)} %get-tuple-element.10), channel_id=1, source_target_pairs={{4,0},{8,4},{12,8},{16,12},{20,16},{24,20},{28,24},{32,28},{36,32}... | collective-permute-start | bytes 393224 | tf_op jit(solution)/shard_map/ppermute | solution.py:15
  60.7 0.0 copy-done
  60.7 0.0 collective-permute-done
  60.7 4.1 %collective-permute-done.1 = bf16[4,64,256]{2,1,0:T(8,128)(2,1)S(1)} collective-permute-done((bf16[4,64,256]{2,1,0:T(8,128)(2,1)S(1)}, bf16[4,64,256]{2,1,0:T(8,128)(2,1)S(1)}, u32[]{:S(2)}, u32[]{:S(2)}) %collective-permute-start.1) | collective-permute-done | bytes 131104 | tf_op jit(solution)/shard_map/ppermute | solution.py:15
  64.9 0.1 pad_maximum_fusion
  65.0 0.0 slice-start
  65.0 8.0 %gather_fusion = bf16[192,64,256]{2,1,0:T(8,128)(2,1)} fusion(bf16[24,64,256]{2,1,0:T(8,128)(2,1)S(1)} %pad_maximum_fusion, s32[1024]{0:T(1024)S(1)} %pad_clamp_fusion), kind=kCustom, calls=%fused_computation | custom fusion | bytes 12583680 | tf_op jit(solution)/shard_map/gather | solution.py:47
  73.0 0.0 slice-start.1
  73.0 6.6 %copy_convert_fusion = f32[192,64,256]{2,0,1:T(8,128)S(1)} fusion(bf16[192,64,256]{2,1,0:T(8,128)(2,1)} %gather_fusion), kind=kLoop, calls=%fused_computation.2 | loop fusion | flops 3145728 | bytes 18874368 | tf_op jit(solution)/shard_map/convert_element_type | solution.py:54
  79.6 0.0 slice-done
  79.6 0.0 slice-done.1
  79.7 5.9 %subtract_convert_fusion = (bf16[192,64,128]{2,0,1:T(8,128)(2,1)}, bf16[192,64,128]{2,0,1:T(8,128)(2,1)}) fusion(f32[192,64,128]{2,0,1:T(8,128)S(1)} %bitcast.39, f32[192,64,128]{2,0,1:T(8,128)} %get-tuple-element.8, f32[192,64,256]{2,0,1:T(8,128)S(1)} %copy_convert_fusion), kind=kLoop, calls=%fused_computation.4 | loop fusion | flops 12582912 | bytes 31457280 | tf_op jit(solution)/shard_map/convert
  85.5 3.8 %maximum_bitcast_fusion = bf16[64,24,8,256]{3,2,1,0:T(8,128)(2,1)S(1)} fusion(bf16[192,64,128]{2,0,1:T(8,128)(2,1)} %get-tuple-element.6, bf16[192,64,128]{2,0,1:T(8,128)(2,1)} %get-tuple-element.5), kind=kLoop, calls=%fused_computation.1 | loop fusion | flops 12582912 | bytes 12582912
  89.3 3.4 %copy.15 = bf16[64,24,8,256]{3,2,0,1:T(8,128)(2,1)} copy(bf16[64,24,8,256]{3,2,1,0:T(8,128)(2,1)S(1)} %maximum_bitcast_fusion) | data formatting | bytes 12582912 | tf_op jit(solution)/shard_map/convert_element_type | solution.py:54
  92.7 47.5 %all-gather.2.cloned.1.call-done = bf16[16384,512]{1,0:T(8,128)(2,1)} async-done(((bf16[64,512]{1,0:T(8,128)(2,1)}), bf16[16384,512]{1,0:T(8,128)(2,1)}) %all-gather.2.cloned.1.call-update) | async-done | bytes 16777232 | tf_op jit(solution)/shard_map/all_gather | solution.py:58
  140.2 11.7 %fusion = bf16[192,512]{1,0:T(8,128)(2,1)} fusion(bf16[192,16384]{1,0:T(8,128)(2,1)} %bitcast.40, bf16[16384,512]{1,0:T(8,128)(2,1)} %all-gather.2.cloned.1.call-done, pred[192]{0:T(512)(128)(4,1)S(1)} %broadcast_compare_fusion.2), kind=kOutput, calls=%fused_computation.6 | convolution fusion | flops 3221422080 | bytes 23265472 | tf_op jit(solution)/shard_map/dot_general | solution.py:56
  (4 shorter events, 0.0 us)
Async XLA Ops:
  6.5 133.7 %all-gather.2.cloned.1.call-start = ((), (), s32[]{:S(2)}) async-start(), calls=%async_computation.1 | async-start | bytes 16842752 | tf_op jit(solution)/shard_map/all_gather | solution.py:58
  10.8 43.4 %all-to-all-start = ((bf16[64,2,2048]{2,1,0:T(2,128)(2,1)}), bf16[64,2,2048]{2,1,0:T(2,128)(2,1)S(1)}, u32[]{:S(2)}, u32[]{:S(2)}) async-start(bf16[64,2,2048]{2,1,0:T(2,128)(2,1)} %reshape.23), calls=%async_computation | async-start | bytes 1048576 | tf_op jit(solution)/shard_map/all_to_all | solution.py:44
  24.5 36.2 %copy-start = (s32[192]{0:T(256)S(1)}, s32[192]{0:T(256)}, u32[]{:S(2)}) copy-start(s32[192]{0:T(256)} %param.7) | copy-start | bytes 2308
  55.0 5.7 %collective-permute-start = (bf16[4,64,256]{2,1,0:T(8,128)(2,1)S(1)}, bf16[4,64,256]{2,1,0:T(8,128)(2,1)S(1)}, u32[]{:S(2)}, u32[]{:S(2)}) collective-permute-start(bf16[4,64,256]{2,1,0:T(8,128)(2,1)S(1)} %get-tuple-element.9), channel_id=1, source_target_pairs={{0,4},{4,8},{8,12},{12,16},{16,20},{20,24},{24,28},{28,32},{32,36}... | collective-permute-start | bytes 393224 | tf_op jit(solution)/shard_map/ppermute | solution.py:14
  58.6 6.3 %collective-permute-start.1 = (bf16[4,64,256]{2,1,0:T(8,128)(2,1)S(1)}, bf16[4,64,256]{2,1,0:T(8,128)(2,1)S(1)}, u32[]{:S(2)}, u32[]{:S(2)}) collective-permute-start(bf16[4,64,256]{2,1,0:T(8,128)(2,1)S(1)} %get-tuple-element.10), channel_id=1, source_target_pairs={{4,0},{8,4},{12,8},{16,12},{20,16},{24,20},{28,24},{32,28},{36,32}... | collective-permute-start | bytes 393224 | tf_op jit(solution)/shard_map/ppermute | solution.py:15
  65.0 14.7 %slice-start = ((s8[6291456]{0:T(1024)(128)(4,1)}), s8[2097152]{0:T(1024)(128)(4,1)S(1)}, s32[]{:S(2)}) async-start(s8[6291456]{0:T(1024)(128)(4,1)} %bitcast.38), calls=%async_computation.2 | async-start | bytes 4194304
  73.0 6.6 %slice-start.1 = ((s8[6291456]{0:T(1024)(128)(4,1)}), s8[4194304]{0:T(1024)(128)(4,1)S(1)}, s32[]{:S(2)}) async-start(s8[6291456]{0:T(1024)(128)(4,1)} %bitcast.38), calls=%async_computation.3 | async-start | bytes 8388608
Sparse Core Ops, SparseCore 0:
  11.0 129.1 all-gather.1
where the time goes:
time: 159 us
  waiting for transfers between devices  52.4 us (33%)
  matrix products  41.4 us (26%)
  other arithmetic  19.1 us (12%)
  starting transfers between devices  18.6 us (12%)
  local copies, waits for them, and re-layouts  13.7 us (9%)
  between operations  13.6 us (9%)
    all_gather x1, waiting for transfers between devices, on_device(): lax.all_gather(wedge_ops, ('dir', 'box'), axis=0, tiled=True)  47.5 us
    dot_general x1, matrix products, on_device(): jnp.dot(selector, angle_table, precision=lax.Precision.HIGHEST)  29.7 us
    all_to_all x1, starting transfers between devices, on_device(): lax.all_to_all(wedge_local, 'dir', split_axis=0, concat_axis=1, tiled=True)  13 us
    dot_general x1, matrix products, on_device(): jnp.dot(operand, lax.all_gather(wedge_ops, ('dir', 'box'), axis=0, tiled=...  11.7 us
    gather x1, local copies, waits for them, and re-layouts, on_device(): picked = widened[local_parent]  8.02 us
    convert_element_type x1, other arithmetic, on_device(): picked.astype(jnp.float32)  6.61 us
    another operation x1, other arithmetic  5.88 us
    unnamed x3, other arithmetic  5.84 us
  transfers between devices with their start and end apart: 4, of which 2 were waited for; matrix products, arithmetic and copies ran while one was open for 39% of the time, Pallas kernels for 0%

commit v1 on v0

v1 whole, which is shorter than its diff:
```python
import functools

import jax
import jax.numpy as jnp
from jax import lax
from jax.experimental import pallas as pl
from jax.experimental.pallas import tpu as pltpu
from jax.sharding import PartitionSpec as P

MESH = pl.DeviceIdType.MESH
NX, NZ, NC, NY = 4, 8, 2, 4
PAR = 16
HALO = 4
WIN = PAR + 2 * HALO
Q = 2


def kernel(ang_ref, a_ref, b_ref, out_ref, cs_ref, sn_ref, e_ref, abuf, op, bbuf, own, cpart, crecv, win,
           la_sem, lb_sem, as_sem, ar_sem, xs_sem, xr_sem, ys_sem, yr_sem, fs_sem, fr_sem,
           cs_sem, cr_sem, hs_sem, hr_sem):
    d = lax.axis_index("dir")
    y = lax.axis_index("box")
    c = d % NC
    z = (d // NC) % NZ
    x = d // (NC * NZ)
    cols = op.shape[1] // (NX * NC)
    wide = bbuf.shape[-1]
    half = cols // 2
    rows = PAR * 8

    def dev(dx=0, dy=0, dz=0, dc=0):
        return ((((x + dx) % NX) * NZ + (z + dz) % NZ) * NC + (c + dc) % NC, (y + dy) % NY)

    lower = ((d + NX * NZ * NC - 1) % (NX * NZ * NC), y)
    upper = ((d + 1) % (NX * NZ * NC), y)
    corner = ((d + NX * NZ * NC - 1 + 2 * c) % (NX * NZ * NC), y)
    sibling = dev(dc=1)

    barrier = pltpu.get_barrier_semaphore()
    peers = [dev(dx=i, dc=j) for i in range(NX) for j in range(NC) if i or j]
    peers += [dev(dy=i) for i in range(1, NY)]
    peers += [dev(dz=i) for i in range(1, NZ)]
    peers += [corner]
    for p in peers:
        pl.semaphore_signal(barrier, inc=1, device_id=p, device_id_type=MESH)

    def remote(src, dst, send, recv, to):
        return pltpu.make_async_remote_copy(
            src_ref=src, dst_ref=dst, send_sem=send, recv_sem=recv, device_id=to, device_id_type=MESH)

    sent = []

    def push(*args):
        copy = remote(*args)
        copy.start()
        sent.append(copy)

    def arrived(ref, sem):
        remote(ref, ref, sem, sem, sibling).wait_recv()

    me = x * NC + c
    own_a = pltpu.make_async_copy(a_ref.at[x, :, c], abuf.at[me], la_sem)
    own_a.start()
    own_b = [pltpu.make_async_copy(b_ref.at[:, pl.ds(q * wide, wide)], bbuf.at[q, x, c, y], lb_sem.at[q])
             for q in range(Q)]
    for copy in own_b:
        copy.start()

    e_ref[...] = (lax.broadcasted_iota(jnp.int32, e_ref.shape, 0) // 8
                  == lax.broadcasted_iota(jnp.int32, e_ref.shape, 1)).astype(e_ref.dtype)
    for i in range(NX):
        for j in range(NC):
            angle = ang_ref[:, pl.ds(i * NZ * NC + z * NC + j, 1), :].reshape(8, half)
            cs_ref[i * NC + j] = jnp.cos(angle)
            sn_ref[i * NC + j] = jnp.sin(angle)

    pl.semaphore_wait(barrier, len(peers))

    def send_own(q):
        block = b_ref.at[:, pl.ds(q * wide, wide)]
        for i in (1, 3, 2):
            push(block, bbuf.at[q, x, c, y], xs_sem.at[q, i], xr_sem.at[q, i], dev(dx=i))
        for i in (1, 3, 2):
            push(block, bbuf.at[q, x, c, y], ys_sem.at[q, 0, i], yr_sem.at[q, 0, i], dev(dy=i))

    send_own(0)
    for i in (2, 1, 3, 0):
        for j in range(NC):
            if i or j:
                push(a_ref.at[(x + i) % NX, :, (c + j) % NC], abuf.at[me],
                     as_sem.at[i * NC + j], ar_sem.at[i * NC + j], dev(dx=i, dc=j))
    send_own(1)

    def spread(q):
        for i in (1, 3, 2):
            slot = bbuf.at[q, (x + NX - i) % NX, c, y]
            arrived(slot, xr_sem.at[q, i])
            for k in (1, 3, 2):
                push(slot, slot, ys_sem.at[q, i, k], yr_sem.at[q, i, k], dev(dy=k))
        own_b[q].wait()
        group = bbuf.at[q, :, c, y]
        push(group, group, fs_sem.at[q, 0], fr_sem.at[q, 0], sibling)

    def collect(q):
        for k in (1, 3, 2):
            group = bbuf.at[q, :, c, (y + NY - k) % NY]
            for i in range(NX):
                arrived(bbuf.at[q, (x + NX - i) % NX, c, (y + NY - k) % NY], yr_sem.at[q, i, k])
            push(group, group, fs_sem.at[q, k], fr_sem.at[q, k], sibling)
        for k in range(NY):
            arrived(bbuf.at[q, :, (c + 1) % NC, (y + NY - k) % NY], fr_sem.at[q, k])

    def turn(k):
        wedge = abuf[k].reshape(rows, cols)
        values = jnp.dot(e_ref[...], wedge, preferred_element_type=jnp.float32).reshape(rows, 8, cols)
        re, im = values[..., :half], values[..., half:]
        cosine, sine = cs_ref[k][None], sn_ref[k][None]
        place = pl.multiple_of(k * cols, cols)
        op[:, pl.ds(place, half)] = (re * cosine - im * sine).astype(op.dtype).reshape(rows * 8, half)
        op[:, pl.ds(place + half, half)] = (re * sine + im * cosine).astype(op.dtype).reshape(rows * 8, half)

    spread(0)
    own_a.wait()
    turn(me)
    for i in (0, 1, 3, 2):
        for j in range(NC):
            if i or j:
                k = ((x + NX - i) % NX) * NC + (c + j) % NC
                arrived(abuf.at[k], ar_sem.at[i * NC + j])
                turn(k)
    spread(1)

    def multiply(q):
        weights = bbuf[q].reshape(op.shape[1], wide)
        for i in (2, 1, 3, 0):
            pair = (z // 2 + i) % (NZ // 2)
            lines = op[pl.ds(pl.multiple_of(pair * 2 * rows, 2 * rows), 2 * rows), :]
            part = jnp.dot(lines, weights, preferred_element_type=jnp.float32)
            if i == 0:
                own[q] = part.reshape(2, rows, wide)
            cpart[q, pair] = part.astype(cpart.dtype).reshape(2, rows, wide)
            for k in range(2):
                if i:
                    to = pair * 2 + k
                    push(cpart.at[q, pair, k], crecv.at[q, z], cs_sem.at[q, i, k], cr_sem.at[q, z],
                         ((x * NZ + to) * NC + c, y))
                elif k:
                    to = z + 1 - 2 * (z % 2)
                    push(cpart.at[q, pair, to % 2], crecv.at[q, z], cs_sem.at[q, 0, 1], cr_sem.at[q, z],
                         ((x * NZ + to) * NC + c, y))

    def total(q):
        value = own[q, z % 2]
        for i in (1, 7, 2, 6, 3, 5, 4):
            src = (z + i) % NZ
            arrived(crecv.at[q, src], cr_sem.at[q, src])
            value = value + crecv[q, src].astype(jnp.float32)
        here = pl.ds(q * wide, wide)
        edge = HALO * 8
        win[pl.ds(edge, rows), here] = value.astype(win.dtype)
        push(win.at[pl.ds(edge, edge), here], win.at[pl.ds(edge + rows, edge), here],
             hs_sem.at[q, 0], hr_sem.at[q, 0], lower)
        push(win.at[pl.ds(rows, edge), here], win.at[pl.ds(0, edge), here],
             hs_sem.at[q, 1], hr_sem.at[q, 1], upper)

    for q in range(Q):
        collect(q)
        multiply(q)
    for q in range(Q):
        total(q)
    edge = HALO * 8
    for q in range(Q):
        here = pl.ds(q * wide, wide)
        arrived(win.at[pl.ds(edge + rows, edge), here], hr_sem.at[q, 0])
        arrived(win.at[pl.ds(0, edge), here], hr_sem.at[q, 1])
    out_ref[...] = win[...]
    for copy in sent:
        copy.wait_send()


def exchange(angle, a, b):
    cols, wide = a.shape[-1], b.shape[1] // Q
    rows = PAR * 8
    depth = NX * NC * cols
    dma = pltpu.SemaphoreType.DMA
    bf16, f32 = jnp.bfloat16, jnp.float32
    return pl.pallas_call(
        kernel,
        out_shape=jax.ShapeDtypeStruct((WIN * 8, b.shape[1]), bf16),
        in_specs=[pl.BlockSpec(memory_space=pltpu.VMEM), pl.BlockSpec(memory_space=pl.ANY),
                  pl.BlockSpec(memory_space=pl.ANY)],
        out_specs=pl.BlockSpec(memory_space=pltpu.VMEM),
        scratch_shapes=[
            pltpu.VMEM((NX * NC, 8, cols // 2), f32),
            pltpu.VMEM((NX * NC, 8, cols // 2), f32),
            pltpu.VMEM((rows * 8, rows), bf16),
            pltpu.VMEM((NX * NC, NZ, PAR, cols), bf16),
            pltpu.VMEM((rows * 8, depth), bf16),
            pltpu.VMEM((Q, NX, NC, NY, cols // NY, wide), bf16),
            pltpu.VMEM((Q, 2, rows, wide), f32),
            pltpu.VMEM((Q, NZ // 2, 2, rows, wide), bf16),
            pltpu.VMEM((Q, NZ, rows, wide), bf16),
            pltpu.VMEM((WIN * 8, b.shape[1]), bf16),
            dma, dma((Q,)),
            dma((NX * NC,)), dma((NX * NC,)),
            dma((Q, NX)), dma((Q, NX)),
            dma((Q, NX, NY)), dma((Q, NX, NY)),
            dma((Q, NY)), dma((Q, NY)),
            dma((Q, NZ // 2, 2)), dma((Q, NZ)),
            dma((Q, 2)), dma((Q, 2)),
        ],
        compiler_params=pltpu.CompilerParams(
            collective_id=0, has_side_effects=True, vmem_limit_bytes=40 * 1024 * 1024),
    )(angle, a, b)


def on_device(wedge_local, wedge_ops, octant_angle, child_box):
    a = wedge_local.reshape(NX, NZ, NC, PAR, wedge_local.shape[-1])
    window = exchange(octant_angle, a, wedge_ops)
    block = lax.axis_index("box") * (NX * NZ * NC) + lax.axis_index("dir")
    first = (block * PAR - HALO) * 8
    place = jnp.where(child_box >= 0, child_box - first, -1)
    pick = (place[:, None] == jnp.arange(WIN * 8, dtype=jnp.int32)[None, :]).astype(jnp.bfloat16)
    return jnp.dot(pick, window, preferred_element_type=jnp.float32).astype(jnp.bfloat16)


def solution(mesh):
    placed = (P("box", "dir", None), P(("dir", "box"), None), P(), P(("box", "dir")))
    return jax.shard_map(
        on_device, mesh=mesh, in_specs=placed, out_specs=P(("box", "dir"), None), check_vma=False
    )
```

time: 159 us -> 58.1 us (0.37)
  Pallas kernels: 0 us -> 53.4 us
  waiting for transfers between devices: 52.4 us -> 0 us
  matrix products: 41.4 us -> 0.93 us
  other arithmetic: 19.1 us -> 0.01 us
  starting transfers between devices: 18.6 us -> 0 us
  between operations: 13.6 us -> 0.01 us
  local copies, waits for them, and re-layouts: 13.7 us -> 3.51 us
    pallas_call x0 -> x1, Pallas kernels: none -> 53.4 us  [exchange(): pl.pallas_call(kernel, out_shape=jax.ShapeDtypeStruct((WIN * 8, b.shape[1...]
    all_gather x1 -> x0, waiting for transfers between devices: 47.5 us -> none  [on_device(): lax.all_gather(wedge_ops, ('dir', 'box'), axis=0, tiled=True)]
    dot_general x2 -> x1, matrix products: 41.4 us -> 0.93 us  [on_device(): jnp.dot(pick, window, preferred_element_type=jnp.float32)]
    all_to_all x1 -> x0, starting transfers between devices: 13 us -> none  [on_device(): lax.all_to_all(wedge_local, 'dir', split_axis=0, concat_axis=1, tiled=True)]
    gather x1 -> x0, local copies, waits for them, and re-layouts: 8.02 us -> none  [on_device(): picked = widened[local_parent]]
    convert_element_type x1 -> x0, other arithmetic: 6.61 us -> none  [on_device(): picked.astype(jnp.float32)]
    another operation x1 -> x0, other arithmetic: 5.88 us -> none
    unnamed x3 -> x0, other arithmetic: 5.84 us -> none
  transfers between devices with their start and end apart: 4 -> 0, of which waited for: 2 -> 0; matrix products, arithmetic and copies ran while one was open for 39% -> 0% of each run, Pallas kernels for 0% -> 0%
where the time goes in v1:
time: 58.1 us; the launch traced here: 57.9 us
  Pallas kernels  53.4 us (92%)
  local copies, waits for them, and re-layouts  3.51 us (6%)
  matrix products  0.93 us (2%)
    pallas_call x1, Pallas kernels, exchange(): pl.pallas_call(kernel, out_shape=jax.ShapeDtypeStruct((WIN * 8, b.shape[1...  53.4 us
    unnamed x8, local copies, waits for them, and re-layouts  3.51 us

profile of v1, /device:TPU:1, one launch (start us, length us, event | category | flops | bytes accessed | tf_op | source)
XLA Modules:
  0.0 57.9 jit_solution(16057302579408257797)
XLA Ops:
  0.0 0.0 copy-start.3
  0.0 0.7 %copy-done.3 = s32[192]{0:T(256)S(1)} copy-done((s32[192]{0:T(256)S(1)}, s32[192]{0:T(256)}, u32[]{:S(2)}) %copy-start.3) | copy-done | bytes 792
  0.7 0.0 copy-start
  0.7 1.0 %copy-done = bf16[1024,1,256]{2,0,1:T(8,128)(2,1)S(1)} copy-done((bf16[1024,1,256]{2,0,1:T(8,128)(2,1)S(1)}, bf16[1024,1,256]{2,0,1:T(8,128)(2,1)}, u32[]{:S(2)}) %copy-start) | copy-done | bytes 524312
  1.7 0.0 copy-start.1
  1.7 0.9 %copy-done.1 = f32[8,64,128]{2,1,0:T(8,128)S(1)} copy-done((f32[8,64,128]{2,1,0:T(8,128)S(1)}, f32[8,64,128]{2,1,0:T(8,128)}, u32[]{:S(2)}) %copy-start.1) | copy-done | bytes 262168
  2.7 0.0 copy-start.2
  2.7 0.8 %copy-done.2 = bf16[64,512]{1,0:T(8,128)(2,1)S(1)} copy-done((bf16[64,512]{1,0:T(8,128)(2,1)S(1)}, bf16[64,512]{1,0:T(8,128)(2,1)}, u32[]{:S(2)}) %copy-start.2) | copy-done | bytes 65560
  3.5 53.4 %shard_map.46 = bf16[192,512]{1,0:T(8,128)(2,1)S(1)} custom-call(f32[8,64,128]{2,1,0:T(8,128)S(1)} %copy-done.1, bf16[4,8,2,16,256]{4,3,2,1,0:T(8,128)(2,1)S(1)} %bitcast.2, bf16[64,512]{1,0:T(8,128)(2,1)S(1)} %copy-done.2), custom_call_target="tpu_custom_call" | custom-call | tf_op jit(solution)/shard_map/pallas_call | solution.py:187
  56.9 0.9 %convolution_convert_fusion = bf16[192,512]{1,0:T(8,128)(2,1)} fusion(bf16[192,512]{1,0:T(8,128)(2,1)S(1)} %shard_map.46, s32[192]{0:T(256)S(1)} %compare_select_fusion), kind=kOutput, calls=%fused_computation | convolution fusion | flops 37883904 | bytes 393984 | tf_op jit(solution)/shard_map/dot_general | solution.py:224
  (1 shorter events, 0.0 us)
Async XLA Ops:
  0.0 0.7 %copy-start.3 = (s32[192]{0:T(256)S(1)}, s32[192]{0:T(256)}, u32[]{:S(2)}) copy-start(s32[192]{0:T(256)} %param.7) | copy-start | bytes 2308
  0.7 1.0 %copy-start = (bf16[1024,1,256]{2,0,1:T(8,128)(2,1)S(1)}, bf16[1024,1,256]{2,0,1:T(8,128)(2,1)}, u32[]{:S(2)}) copy-start(bf16[1024,1,256]{2,0,1:T(8,128)(2,1)} %param.4) | copy-start | bytes 1572868
  1.7 0.9 %copy-start.1 = (f32[8,64,128]{2,1,0:T(8,128)S(1)}, f32[8,64,128]{2,1,0:T(8,128)}, u32[]{:S(2)}) copy-start(f32[8,64,128]{2,1,0:T(8,128)} %ang_ref.1) | copy-start | bytes 786436
  2.7 0.8 %copy-start.2 = (bf16[64,512]{1,0:T(8,128)(2,1)S(1)}, bf16[64,512]{1,0:T(8,128)(2,1)}, u32[]{:S(2)}) copy-start(bf16[64,512]{1,0:T(8,128)(2,1)} %b_ref.1) | copy-start | bytes 196612

commit v2 on v1

v2 whole, which is shorter than its diff:
```python
import functools

import jax
import jax.numpy as jnp
from jax import lax
from jax.experimental import pallas as pl
from jax.experimental.pallas import tpu as pltpu
from jax.sharding import PartitionSpec as P

MESH = pl.DeviceIdType.MESH
NX, NZ, NC, NY = 4, 8, 2, 4
PAR = 16
HALO = 4
WIN = PAR + 2 * HALO
Q = 2
R = 2


def kernel(ang_hbm, a_ref, b_ref, box_hbm, out_ref, box_ref, ang_ref, cs_ref, sn_ref, e_ref, abuf, op, bbuf, acc, cpart, relay, near, far, mid,
           relayed, win, lc_sem, lg_sem, la_sem, lb_sem, as_sem, ar_sem, xs_sem, xr_sem, ys_sem, yr_sem, fs_sem, fr_sem,
           cs_sem, cr_sem, hs_sem, hr_sem):
    d = lax.axis_index("dir")
    y = lax.axis_index("box")
    c = d % NC
    z = (d // NC) % NZ
    x = d // (NC * NZ)
    cols = op.shape[1] // (NX * NC)
    wide = bbuf.shape[-1]
    half = cols // 2
    edge = HALO * 8
    part = PAR * 8 // R

    def dev(dx=0, dy=0, dz=0, dc=0):
        return ((((x + dx) % NX) * NZ + (z + dz) % NZ) * NC + (c + dc) % NC, (y + dy) % NY)

    lower = ((d + NX * NZ * NC - 1) % (NX * NZ * NC), y)
    upper = ((d + 1) % (NX * NZ * NC), y)
    corner = ((d + NX * NZ * NC - 1 + 2 * c) % (NX * NZ * NC), y)
    sibling = dev(dc=1)

    barrier = pltpu.get_barrier_semaphore()
    peers = [dev(dx=i, dc=j) for i in range(NX) for j in range(NC) if i or j]
    peers += [dev(dy=i) for i in range(1, NY)]
    peers += [dev(dz=i) for i in (1, 2, NZ - 2, NZ - 1)]
    peers += [corner]
    for p in peers:
        pl.semaphore_signal(barrier, inc=1, device_id=p, device_id_type=MESH)

    def remote(src, dst, send, recv, to):
        return pltpu.make_async_remote_copy(
            src_ref=src, dst_ref=dst, send_sem=send, recv_sem=recv, device_id=to, device_id_type=MESH)

    sent = []

    def push(*args):
        copy = remote(*args)
        copy.start()
        sent.append(copy)

    def arrived(ref, sem):
        remote(ref, ref, sem, sem, sibling).wait_recv()

    angles = pltpu.make_async_copy(ang_hbm, ang_ref, lg_sem)
    angles.start()
    boxes = pltpu.make_async_copy(box_hbm, box_ref, lc_sem)
    boxes.start()
    me = x * NC + c
    own_a = pltpu.make_async_copy(a_ref.at[x, :, c], abuf.at[me], la_sem)
    own_a.start()
    own_b = [pltpu.make_async_copy(b_ref.at[:, pl.ds(q * wide, wide)], bbuf.at[q, x, c, y], lb_sem.at[q])
             for q in range(Q)]
    for copy in own_b:
        copy.start()

    pl.semaphore_wait(barrier, len(peers))

    def send_own(q):
        block = b_ref.at[:, pl.ds(q * wide, wide)]
        for i in (2, 1, 3):
            push(block, bbuf.at[q, x, c, y], xs_sem.at[q, i], xr_sem.at[q, i], dev(dx=i))
        for i in (2, 1, 3):
            push(block, bbuf.at[q, x, c, y], ys_sem.at[q, 0, i], yr_sem.at[q, 0, i], dev(dy=i))

    for q in range(Q):
        send_own(q)
    for i in (2, 1, 3, 0):
        for j in range(NC):
            if i or j:
                push(a_ref.at[(x + i) % NX, :, (c + j) % NC], abuf.at[me],
                     as_sem.at[i * NC + j], ar_sem.at[i * NC + j], dev(dx=i, dc=j))

    row = lax.broadcasted_iota(jnp.int32, e_ref.shape, 0)
    place = (row // 8) % (PAR // R)
    place = jnp.where(row < NZ * part, jnp.where(place < HALO, place, place + PAR - 2 * HALO), place + HALO)
    e_ref[...] = ((row // part) % NZ * PAR + place
                  == lax.broadcasted_iota(jnp.int32, e_ref.shape, 1)).astype(e_ref.dtype)
    angles.wait()
    for i in range(NX):
        for j in range(NC):
            angle = ang_ref[:, pl.ds(i * NZ * NC + z * NC + j, 1), :].reshape(8, half)
            cs_ref[i * NC + j] = jnp.cos(angle)
            sn_ref[i * NC + j] = jnp.sin(angle)

    boxes.wait()
    first = ((y * (NX * NZ * NC) + d) * PAR - HALO) * 8
    place = box_ref[...] - first
    place = jnp.where(place < 2 * edge, place, jnp.where(
        place < 4 * edge, place + edge, jnp.where(place < 5 * edge, place - 2 * edge, place)))
    place = jnp.where(box_ref[...] >= 0, place, -1)
    pick = (lax.broadcasted_iota(jnp.int32, (WIN * 8, place.shape[1]), 0) == place).astype(win.dtype)

    def spread(q):
        for i in (1, 3, 2):
            slot = bbuf.at[q, (x + NX - i) % NX, c, y]
            arrived(slot, xr_sem.at[q, i])
            for k in (1, 3, 2):
                push(slot, slot, ys_sem.at[q, i, k], yr_sem.at[q, i, k], dev(dy=k))

    def collect(q, i):
        if i == 0:
            own_b[q].wait()
        for k in (1, 3, 2):
            arrived(bbuf.at[q, (x + NX - i) % NX, c, (y + NY - k) % NY], yr_sem.at[q, i, k])
        group = bbuf.at[q, (x + NX - i) % NX, c]
        push(group, group, fs_sem.at[q, i], fr_sem.at[q, i], sibling)

    def complete(q):
        for i in range(NX):
            arrived(bbuf.at[q, (x + NX - i) % NX, (c + 1) % NC], fr_sem.at[q, i])

    def turn(k, r):
        rows = NZ * part
        wedge = abuf[k].reshape(NZ * PAR, cols)
        chosen = e_ref[pl.ds(r * rows, rows), :]
        values = jnp.dot(chosen, wedge, preferred_element_type=jnp.float32).reshape(rows // 8, 8, cols)
        re, im = values[..., :half], values[..., half:]
        cosine, sine = cs_ref[k][None], sn_ref[k][None]
        column = pl.multiple_of(k * cols, cols)
        lines = pl.ds(r * rows, rows)
        op[lines, pl.ds(column, half)] = (re * cosine - im * sine).astype(op.dtype).reshape(rows, half)
        op[lines, pl.ds(column + half, half)] = (re * sine + im * cosine).astype(op.dtype).reshape(rows, half)

    for q in range(Q):
        spread(q)
    for q in range(Q):
        collect(q, 0)
    collect(0, 1)
    own_a.wait()
    turn(me, 0)
    for i in (0, 1, 3, 2):
        for j in range(NC):
            if i or j:
                k = ((x + NX - i) % NX) * NC + (c + j) % NC
                arrived(abuf.at[k], ar_sem.at[i * NC + j])
                turn(k, 0)

    narrow = wide // 2

    def multiply(q, r):
        lines = op[pl.ds(r * NZ * part, NZ * part), :]
        weights = bbuf[q].reshape(op.shape[1], wide)
        sums = jnp.dot(lines, weights, preferred_element_type=jnp.float32)
        acc[q, r] = sums.reshape(NZ, part, wide)
        cpart[q, r] = sums.astype(cpart.dtype).reshape(NZ, part, wide)
        for s, sign in enumerate((1, -1)):
            push(cpart.at[q, r, (z + NZ + 3 * sign) % NZ], mid.at[q, r, s],
                 cs_sem.at[q, r, 2 + s], cr_sem.at[q, r, 2 + s], dev(dz=NZ + sign))
        for s, sign in enumerate((1, -1)):
            push(cpart.at[q, r, (z + NZ // 2) % NZ, :, pl.ds(s * narrow, narrow)], far.at[q, r, s],
                 cs_sem.at[q, r, 4 + s], cr_sem.at[q, r, 4 + s], dev(dz=NZ + 2 * sign))

    def adjacent(q, r):
        for s, sign in enumerate((1, -1)):
            push(cpart.at[q, r, (z + NZ + sign) % NZ], near.at[q, r, s],
                 cs_sem.at[q, r, s], cr_sem.at[q, r, s], dev(dz=NZ + sign))

    def forward(q, r):
        for s, sign in enumerate((1, -1)):
            arrived(mid.at[q, r, s], cr_sem.at[q, r, 2 + s])
            arrived(far.at[q, r, s], cr_sem.at[q, r, 4 + s])
            value = acc[q, r, (z + NZ + 2 * sign) % NZ] + mid[q, r, s].astype(jnp.float32)
            extra = far[q, r, s].astype(jnp.float32)
            here, other = pl.ds(s * narrow, narrow), pl.ds((1 - s) * narrow, narrow)
            relay[q, r, s, :, here] = (value[:, s * narrow:(s + 1) * narrow] + extra).astype(relay.dtype)
            relay[q, r, s, :, other] = value[:, (1 - s) * narrow:(2 - s) * narrow].astype(relay.dtype)
            push(relay.at[q, r, s], relayed.at[q, r, s],
                 cs_sem.at[q, r, 6 + s], cr_sem.at[q, r, 6 + s], dev(dz=NZ + 2 * sign))

    def total(q, r):
        value = acc[q, r, z]
        for s in range(2):
            arrived(near.at[q, r, s], cr_sem.at[q, r, s])
            value = value + near[q, r, s].astype(jnp.float32)
        for s in range(2):
            arrived(relayed.at[q, r, s], cr_sem.at[q, r, 6 + s])
            value = value + relayed[q, r, s].astype(jnp.float32)
        here = pl.ds(q * wide, wide)
        win[pl.ds(edge + r * part, part), here] = value.astype(win.dtype)
        if r == 0:
            push(win.at[pl.ds(edge, edge), here], win.at[pl.ds(5 * edge, edge), here],
                 hs_sem.at[q, 0], hr_sem.at[q, 0], lower)
            push(win.at[pl.ds(2 * edge, edge), here], win.at[pl.ds(0, edge), here],
                 hs_sem.at[q, 1], hr_sem.at[q, 1], upper)

    collect(0, 3)
    collect(0, 2)
    complete(0)
    multiply(0, 0)
    for k in range(NX * NC):
        turn(k, 1)
    multiply(0, 1)
    adjacent(0, 0)
    for i in (1, 3, 2):
        collect(1, i)
    complete(1)
    multiply(1, 0)
    multiply(1, 1)
    for r in range(R):
        for q in range(Q):
            if q or r:
                adjacent(q, r)
    for r in range(R):
        for q in range(Q):
            forward(q, r)
    for r in range(R):
        for q in range(Q):
            total(q, r)
    for q in range(Q):
        here = pl.ds(q * wide, wide)
        arrived(win.at[pl.ds(5 * edge, edge), here], hr_sem.at[q, 0])
        arrived(win.at[pl.ds(0, edge), here], hr_sem.at[q, 1])
    out_ref[...] = lax.dot_general(
        pick, win[...], (((0,), (0,)), ((), ())), preferred_element_type=jnp.float32).astype(out_ref.dtype)
    for copy in sent:
        copy.wait_send()


def exchange(angle, a, b, boxes):
    cols, wide = a.shape[-1], b.shape[1] // Q
    rows = PAR * 8
    part = rows // R
    depth = NX * NC * cols
    dma = pltpu.SemaphoreType.DMA
    bf16, f32 = jnp.bfloat16, jnp.float32
    return pl.pallas_call(
        kernel,
        out_shape=jax.ShapeDtypeStruct((boxes.shape[1], b.shape[1]), bf16),
        in_specs=[pl.BlockSpec(memory_space=pltpu.HBM)] * 4,
        out_specs=pl.BlockSpec(memory_space=pltpu.VMEM),
        scratch_shapes=[
            pltpu.VMEM(boxes.shape, jnp.int32),
            pltpu.VMEM(angle.shape, f32),
            pltpu.VMEM((NX * NC, 8, cols // 2), f32),
            pltpu.VMEM((NX * NC, 8, cols // 2), f32),
            pltpu.VMEM((rows * NZ, PAR * NZ), bf16),
            pltpu.VMEM((NX * NC, NZ, PAR, cols), bf16),
            pltpu.VMEM((rows * NZ, depth), bf16),
            pltpu.VMEM((Q, NX, NC, NY, cols // NY, wide), bf16),
            pltpu.VMEM((Q, R, NZ, part, wide), f32),
            pltpu.VMEM((Q, R, NZ, part, wide), bf16),
            pltpu.VMEM((Q, R, 2, part, wide), bf16),
            pltpu.VMEM((Q, R, 2, part, wide), bf16),
            pltpu.VMEM((Q, R, 2, part, wide // 2), bf16),
            pltpu.VMEM((Q, R, 2, part, wide), bf16),
            pltpu.VMEM((Q, R, 2, part, wide), bf16),
            pltpu.VMEM((WIN * 8, b.shape[1]), bf16),
            dma, dma, dma, dma((Q,)),
            dma((NX * NC,)), dma((NX * NC,)),
            dma((Q, NX)), dma((Q, NX)),
            dma((Q, NX, NY)), dma((Q, NX, NY)),
            dma((Q, NX)), dma((Q, NX)),
            dma((Q, R, 8)), dma((Q, R, 8)),
            dma((Q, 2)), dma((Q, 2)),
        ],
        compiler_params=pltpu.CompilerParams(
            collective_id=0, has_side_effects=True, vmem_limit_bytes=40 * 1024 * 1024),
    )(*[pltpu.with_memory_space_constraint(v, pltpu.HBM) for v in (angle, a, b, boxes)])


def on_device(wedge_local, wedge_ops, octant_angle, child_box):
    a = wedge_local.reshape(NX, NZ, NC, PAR, wedge_local.shape[-1])
    return exchange(octant_angle, a, wedge_ops, child_box.reshape(1, -1))


def solution(mesh):
    placed = (P("box", "dir", None), P(("dir", "box"), None), P(), P(("box", "dir")))
    return jax.shard_map(
        on_device, mesh=mesh, in_specs=placed, out_specs=P(("box", "dir"), None), check_vma=False
    )
```

time: 58.1 us -> 45.3 us (0.78)
  Pallas kernels: 53.4 us -> 44.6 us
  local copies, waits for them, and re-layouts: 3.51 us -> 0.68 us
  matrix products: 0.93 us -> 0 us
    pallas_call x1, Pallas kernels: 53.4 us -> 44.6 us  [exchange(): pl.pallas_call(kernel, out_shape=jax.ShapeDtypeStruct((boxes.shape[1], b....]
    unnamed x8 -> x1, local copies, waits for them, and re-layouts: 3.51 us -> 0.68 us
    dot_general x1 -> x0, matrix products: 0.93 us -> none  [on_device(): jnp.dot(pick, window, preferred_element_type=jnp.float32)]
where the time goes in v2:
time: 45.3 us; the launch traced here: 45.2 us
  Pallas kernels  44.6 us (98%)
  local copies, waits for them, and re-layouts  0.68 us (2%)
    pallas_call x1, Pallas kernels, exchange(): pl.pallas_call(kernel, out_shape=jax.ShapeDtypeStruct((boxes.shape[1], b....  44.6 us

profile of v2, /device:TPU:1, one launch (start us, length us, event | category | flops | bytes accessed | tf_op | source)
XLA Modules:
  0.0 45.2 jit_solution(12107356155825123097)
XLA Ops:
  0.0 44.6 %shard_map.46 = bf16[192,512]{1,0:T(8,128)(2,1)S(1)} custom-call(f32[8,64,128]{2,1,0:T(8,128)} %ang_hbm.1, bf16[4,8,2,16,256]{4,3,2,1,0:T(8,128)(2,1)} %bitcast.2, bf16[64,512]{1,0:T(8,128)(2,1)} %b_ref.1, s32[1,192]{1,0:T(1,128)} %bitcast.3), custom_call_target="tpu_custom_call" | custom-call | tf_op jit(solution)/shard_map/pallas_call | solution.py:245
  44.6 0.7 %copy.6 = bf16[192,512]{1,0:T(8,128)(2,1)} copy(bf16[192,512]{1,0:T(8,128)(2,1)S(1)} %shard_map.46) | data formatting | bytes 393216

commit v3 on v2

--- a/solution.py
+++ b/solution.py
@@ -1,5 +1,3 @@
-import functools
-
 import jax
 import jax.numpy as jnp
 from jax import lax
@@ -154,7 +152,7 @@
                 arrived(abuf.at[k], ar_sem.at[i * NC + j])
                 turn(k, 0)
 
-    narrow = wide // 2
+    low = part // 2
 
     def multiply(q, r):
         lines = op[pl.ds(r * NZ * part, NZ * part), :]
@@ -166,7 +164,7 @@
             push(cpart.at[q, r, (z + NZ + 3 * sign) % NZ], mid.at[q, r, s],
                  cs_sem.at[q, r, 2 + s], cr_sem.at[q, r, 2 + s], dev(dz=NZ + sign))
         for s, sign in enumerate((1, -1)):
-            push(cpart.at[q, r, (z + NZ // 2) % NZ, :, pl.ds(s * narrow, narrow)], far.at[q, r, s],
+            push(cpart.at[q, r, (z + NZ // 2) % NZ, pl.ds(s * low, low)], far.at[q, r, s],
                  cs_sem.at[q, r, 4 + s], cr_sem.at[q, r, 4 + s], dev(dz=NZ + 2 * sign))
 
     def adjacent(q, r):
@@ -180,9 +178,9 @@
             arrived(far.at[q, r, s], cr_sem.at[q, r, 4 + s])
             value = acc[q, r, (z + NZ + 2 * sign) % NZ] + mid[q, r, s].astype(jnp.float32)
             extra = far[q, r, s].astype(jnp.float32)
-            here, other = pl.ds(s * narrow, narrow), pl.ds((1 - s) * narrow, narrow)
-            relay[q, r, s, :, here] = (value[:, s * narrow:(s + 1) * narrow] + extra).astype(relay.dtype)
-            relay[q, r, s, :, other] = value[:, (1 - s) * narrow:(2 - s) * narrow].astype(relay.dtype)
+            here, other = pl.ds(s * low, low), pl.ds((1 - s) * low, low)
+            relay[q, r, s, here] = (value[s * low:(s + 1) * low] + extra).astype(relay.dtype)
+            relay[q, r, s, other] = value[(1 - s) * low:(2 - s) * low].astype(relay.dtype)
             push(relay.at[q, r, s], relayed.at[q, r, s],
                  cs_sem.at[q, r, 6 + s], cr_sem.at[q, r, 6 + s], dev(dz=NZ + 2 * sign))
 
@@ -214,17 +212,16 @@
         collect(1, i)
     complete(1)
     multiply(1, 0)
+    adjacent(0, 1)
     multiply(1, 1)
-    for r in range(R):
-        for q in range(Q):
-            if q or r:
-                adjacent(q, r)
-    for r in range(R):
-        for q in range(Q):
-            forward(q, r)
-    for r in range(R):
-        for q in range(Q):
-            total(q, r)
+    order = [(q, r) for r in range(R) for q in range(Q)]
+    for q, r in order:
+        if q:
+            adjacent(q, r)
+    for q, r in order:
+        forward(q, r)
+    for q, r in order:
+        total(q, r)
     for q in range(Q):
         here = pl.ds(q * wide, wide)
         arrived(win.at[pl.ds(5 * edge, edge), here], hr_sem.at[q, 0])
@@ -260,7 +257,7 @@
             pltpu.VMEM((Q, R, NZ, part, wide), bf16),
             pltpu.VMEM((Q, R, 2, part, wide), bf16),
             pltpu.VMEM((Q, R, 2, part, wide), bf16),
-            pltpu.VMEM((Q, R, 2, part, wide // 2), bf16),
+            pltpu.VMEM((Q, R, 2, part // 2, wide), bf16),
             pltpu.VMEM((Q, R, 2, part, wide), bf16),
             pltpu.VMEM((Q, R, 2, part, wide), bf16),
             pltpu.VMEM((WIN * 8, b.shape[1]), bf16),

time: 45.3 us -> 45 us (level)
  no operation moved by 1% of the time
where the time goes in v3:
time: 45 us
  Pallas kernels  44.3 us (98%)
  local copies, waits for them, and re-layouts  0.68 us (2%)
    pallas_call x1, Pallas kernels, exchange(): pl.pallas_call(kernel, out_shape=jax.ShapeDtypeStruct((boxes.shape[1], b....  44.3 us

profile of v3, /device:TPU:1, one launch (start us, length us, event | category | flops | bytes accessed | tf_op | source)
XLA Modules:
  0.0 45.0 jit_solution(8503584819750125607)
XLA Ops:
  0.0 44.3 %shard_map.46 = bf16[192,512]{1,0:T(8,128)(2,1)S(1)} custom-call(f32[8,64,128]{2,1,0:T(8,128)} %ang_hbm.1, bf16[4,8,2,16,256]{4,3,2,1,0:T(8,128)(2,1)} %bitcast.2, bf16[64,512]{1,0:T(8,128)(2,1)} %b_ref.1, s32[1,192]{1,0:T(1,128)} %bitcast.3), custom_call_target="tpu_custom_call" | custom-call | tf_op jit(solution)/shard_map/pallas_call | solution.py:242
  44.3 0.7 %copy.6 = bf16[192,512]{1,0:T(8,128)(2,1)} copy(bf16[192,512]{1,0:T(8,128)(2,1)S(1)} %shard_map.46) | data formatting | bytes 393216

commit v4 on v3

--- a/solution.py
+++ b/solution.py
@@ -208,16 +208,15 @@
         turn(k, 1)
     multiply(0, 1)
     adjacent(0, 0)
+    adjacent(0, 1)
     for i in (1, 3, 2):
         collect(1, i)
     complete(1)
     multiply(1, 0)
-    adjacent(0, 1)
+    adjacent(1, 0)
     multiply(1, 1)
+    adjacent(1, 1)
     order = [(q, r) for r in range(R) for q in range(Q)]
-    for q, r in order:
-        if q:
-            adjacent(q, r)
     for q, r in order:
         forward(q, r)
     for q, r in order:

time: 45 us -> 44.4 us (0.987)
  Pallas kernels: 44.3 us -> 43.6 us
    pallas_call x1, Pallas kernels: 44.3 us -> 43.6 us  [exchange(): pl.pallas_call(kernel, out_shape=jax.ShapeDtypeStruct((boxes.shape[1], b....]
where the time goes in v4:
time: 44.4 us; the launch traced here: 44.3 us
  Pallas kernels  43.6 us (98%)
  local copies, waits for them, and re-layouts  0.68 us (2%)
    pallas_call x1, Pallas kernels, exchange(): pl.pallas_call(kernel, out_shape=jax.ShapeDtypeStruct((boxes.shape[1], b....  43.6 us

profile of v4, /device:TPU:1, one launch (start us, length us, event | category | flops | bytes accessed | tf_op | source)
XLA Modules:
  0.0 44.3 jit_solution(11971806162887584747)
XLA Ops:
  0.0 43.6 %shard_map.46 = bf16[192,512]{1,0:T(8,128)(2,1)S(1)} custom-call(f32[8,64,128]{2,1,0:T(8,128)} %ang_hbm.1, bf16[4,8,2,16,256]{4,3,2,1,0:T(8,128)(2,1)} %bitcast.2, bf16[64,512]{1,0:T(8,128)(2,1)} %b_ref.1, s32[1,192]{1,0:T(1,128)} %bitcast.3), custom_call_target="tpu_custom_call" | custom-call | tf_op jit(solution)/shard_map/pallas_call | solution.py:241
  43.6 0.7 %copy.6 = bf16[192,512]{1,0:T(8,128)(2,1)} copy(bf16[192,512]{1,0:T(8,128)(2,1)S(1)} %shard_map.46) | data formatting | bytes 393216

commit v5 on v4

--- a/solution.py
+++ b/solution.py
@@ -72,15 +72,13 @@
 
     pl.semaphore_wait(barrier, len(peers))
 
-    def send_own(q):
-        block = b_ref.at[:, pl.ds(q * wide, wide)]
+    blocks = [b_ref.at[:, pl.ds(q * wide, wide)] for q in range(Q)]
+    for q in range(Q):
         for i in (2, 1, 3):
-            push(block, bbuf.at[q, x, c, y], xs_sem.at[q, i], xr_sem.at[q, i], dev(dx=i))
+            push(blocks[q], bbuf.at[q, x, c, y], xs_sem.at[q, i], xr_sem.at[q, i], dev(dx=i))
+    for q in range(Q):
         for i in (2, 1, 3):
-            push(block, bbuf.at[q, x, c, y], ys_sem.at[q, 0, i], yr_sem.at[q, 0, i], dev(dy=i))
-
-    for q in range(Q):
-        send_own(q)
+            push(blocks[q], bbuf.at[q, x, c, y], ys_sem.at[q, 0, i], yr_sem.at[q, 0, i], dev(dy=i))
     for i in (2, 1, 3, 0):
         for j in range(NC):
             if i or j:

time: 44.4 us -> 44.4 us (level)
  no operation moved by 1% of the time
where the time goes in v5:
time: 44.4 us; the launch traced here: 44.3 us
  Pallas kernels  43.6 us (98%)
  local copies, waits for them, and re-layouts  0.68 us (2%)
    pallas_call x1, Pallas kernels, exchange(): pl.pallas_call(kernel, out_shape=jax.ShapeDtypeStruct((boxes.shape[1], b....  43.6 us

profile of v5, /device:TPU:1, one launch (start us, length us, event | category | flops | bytes accessed | tf_op | source)
XLA Modules:
  0.0 44.3 jit_solution(17279892269794592320)
XLA Ops:
  0.0 43.6 %shard_map.46 = bf16[192,512]{1,0:T(8,128)(2,1)S(1)} custom-call(f32[8,64,128]{2,1,0:T(8,128)} %ang_hbm.1, bf16[4,8,2,16,256]{4,3,2,1,0:T(8,128)(2,1)} %bitcast.2, bf16[64,512]{1,0:T(8,128)(2,1)} %b_ref.1, s32[1,192]{1,0:T(1,128)} %bitcast.3), custom_call_target="tpu_custom_call" | custom-call | tf_op jit(solution)/shard_map/pallas_call | solution.py:239
  43.6 0.7 %copy.6 = bf16[192,512]{1,0:T(8,128)(2,1)} copy(bf16[192,512]{1,0:T(8,128)(2,1)S(1)} %shard_map.46) | data formatting | bytes 393216
